TPU v7x, 128 devices: a whole 4x4x4 slice. The times are simulated.
128 devices in a mesh: segment: 8 (over y_lo, z), dp: 16 (over y_hi, x, core).
Axes of the slice: x: 4, y: 4 (y_hi: 2, y_lo: 2; y = y_hi * 2 + y_lo), z: 4, core: 2. Of those that a mesh axis runs over, the one named last changes fastest.
Arguments:
- tokens: bfloat16 [4, 512, 6144], P(None, 'dp'), may hold values from -18 to 18
- norm_gain: bfloat16 [6144], replicated, may hold values from 0.099609375 to 1.8984375
- router_weight: bfloat16 [6144, 8], replicated, may hold values from -0.078125 to 0.078125
- expert_ids: int32 [4, 512, 2], P(None, 'dp'), may hold values from 0 to 7, all different within a row; in each aligned block of 32 rows (0 to 31, 32 to 63, ..., all dimensions but the last counted through in order) at most 12 rows name the same one
- w_gate: bfloat16 [8, 6144, 8192], P('segment', None, 'dp'), may hold values from -0.078125 to 0.078125
- w_up: bfloat16 [8, 6144, 8192], P('segment', None, 'dp'), may hold values from -0.078125 to 0.078125
- w_down: bfloat16 [8, 8192, 6144], P('segment', 'dp'), may hold values from -0.0625 to 0.0625
Outputs:
- scored: bfloat16 [4, 512, 6144], P(None, 'dp', 'segment')
Inputs may be any that keep to these rules, and one draw needn't show every extreme that they name: `expert_ids`: each token names two different experts. In each micro-batch the 32 rows of one device name each expert at most 12 times, and in every draw some expert is named exactly 12 times by some device's rows.
All inputs are finite; a program needn't handle non-finite values.
Results may differ from a plain program's by a relative error of at most 0.0035.
Values may be sent and summed in bfloat16 or wider, within the bound.
A program may use at most 128 MiB of HBM per device.

v0:
```python
import jax
import jax.numpy as jnp
from jax import lax
from jax.sharding import PartitionSpec as P

epsilon = 1e-05


def rms_normed(tokens, norm_gain):
    widened = tokens.astype(jnp.float32)
    inverse_rms = lax.rsqrt(jnp.mean(widened * widened, axis=-1, keepdims=True) + epsilon)
    return (widened, (widened * inverse_rms * norm_gain.astype(jnp.float32)).astype(jnp.bfloat16))


def pair_gates(pair_ids, logits):
    expert_range = jnp.arange(logits.shape[-1], dtype=jnp.int32)
    first_logit = jnp.sum(jnp.where(pair_ids[..., 0:1] == expert_range, logits, 0.0), axis=-1)
    second_logit = jnp.sum(jnp.where(pair_ids[..., 1:2] == expert_range, logits, 0.0), axis=-1)
    return (jax.nn.sigmoid(first_logit - second_logit), jax.nn.sigmoid(second_logit - first_logit))


def expert_weight(pair_ids, first_gate, second_gate, expert):
    return jnp.where(pair_ids[..., 0] == expert, first_gate, 0.0) + jnp.where(
        pair_ids[..., 1] == expert, second_gate, 0.0
    )


def slot_table(pair_ids, expert, slot_count):
    chosen = jnp.any(pair_ids == expert, axis=-1)
    hit_count = chosen.astype(jnp.int32)
    position = jnp.cumsum(hit_count, axis=-1) - hit_count
    slot_range = jnp.arange(slot_count, dtype=jnp.int32)
    dispatch = chosen[..., None, :] & (position[..., None, :] == slot_range[:, None])
    return (position, dispatch)


def per_device(tokens, norm_gain, router_weight, expert_ids, w_gate, w_up, w_down):
    micro_count, tok_rows, model_width = tokens.shape
    expert_count = router_weight.shape[1]
    slot_count = 2 * tok_rows // expert_count + tok_rows // 8
    segment_count = lax.axis_size("segment")
    segment_index = lax.axis_index("segment")
    slice_width = model_width // segment_count
    gate_matrix = w_gate[0]
    up_matrix = w_up[0]
    down_matrix = w_down[0]
    widened, normed = rms_normed(tokens, norm_gain)
    logits = jnp.dot(
        normed.reshape(-1, model_width), router_weight, preferred_element_type=jnp.float32
    )
    logits = logits.reshape(micro_count, tok_rows, expert_count)
    first_gate, second_gate = pair_gates(expert_ids, logits)
    outputs = []
    positions = []
    for micro_index in range(micro_count):
        position, dispatch = slot_table(expert_ids[micro_index], segment_index, slot_count)
        routed = jnp.dot(
            dispatch.astype(jnp.bfloat16), normed[micro_index], preferred_element_type=jnp.float32
        ).astype(jnp.bfloat16)
        piece_rows = lax.all_gather(routed, "dp", axis=0, tiled=True)
        gate_proj = jnp.dot(piece_rows, gate_matrix, preferred_element_type=jnp.float32)
        up_proj = jnp.dot(piece_rows, up_matrix, preferred_element_type=jnp.float32)
        hidden = (jax.nn.silu(gate_proj) * up_proj).astype(jnp.bfloat16)
        outputs.append(
            lax.psum_scatter(
                jnp.dot(hidden, down_matrix, preferred_element_type=jnp.float32),
                "dp",
                scatter_dimension=0,
                tiled=True,
            )
        )
        positions.append(position)
    own_part = lax.dynamic_slice_in_dim(widened, segment_index * slice_width, slice_width, 2)
    placed = []
    for micro_index in range(micro_count):
        weight = expert_weight(
            expert_ids[micro_index],
            first_gate[micro_index],
            second_gate[micro_index],
            segment_index,
        )
        taken = jnp.take(
            outputs[micro_index], jnp.clip(positions[micro_index], 0, slot_count - 1), axis=0
        )
        placed.append(weight[:, None] * taken)
    summed = lax.psum_scatter(jnp.stack(placed), "segment", scatter_dimension=2, tiled=True)
    return (own_part + summed).astype(jnp.bfloat16)


def solution(mesh):
    placed = (
        P(None, "dp", None),
        P(),
        P(),
        P(None, "dp", None),
        P("segment", None, "dp"),
        P("segment", None, "dp"),
        P("segment", "dp", None),
    )
    return jax.shard_map(
        per_device, mesh=mesh, in_specs=placed, out_specs=P(None, "dp", "segment"), check_vma=False
    )
```

profile of v0, /device:TPU:0, one launch (start us, length us, event | category | flops | bytes accessed | tf_op | source)
XLA Modules:
  0.0 637.2 jit_solution(11767465393413596786)
XLA Ops:
  17.9 50.2 %all-gather.13.cloned.1.call-done = bf16[16,12,6144]{2,1,0:T(8,128)(2,1)} async-done(((bf16[1,12,6144]{2,1,0:T(8,128)(2,1)}), bf16[16,12,6144]{2,1,0:T(8,128)(2,1)}) %all-gather.13.cloned.1.call-update) | async-done | bytes 2359312 | tf_op jit(solution)/shard_map/all_gather | solution.py:60
  68.1 2.9 reshape.195
  70.9 50.7 %all-gather.9.cloned.1.call-done = bf16[16,12,6144]{2,1,0:T(8,128)(2,1)} async-done(((bf16[1,12,6144]{2,1,0:T(8,128)(2,1)}), bf16[16,12,6144]{2,1,0:T(8,128)(2,1)}) %all-gather.9.cloned.1.call-update) | async-done | bytes 2359312 | tf_op jit(solution)/shard_map/all_gather | solution.py:60
  121.6 4.3 reshape.191
  125.9 49.3 %all-gather.11.cloned.1.call-done = bf16[16,12,6144]{2,1,0:T(8,128)(2,1)} async-done(((bf16[1,12,6144]{2,1,0:T(8,128)(2,1)}), bf16[16,12,6144]{2,1,0:T(8,128)(2,1)}) %all-gather.11.cloned.1.call-update) | async-done | bytes 2359312 | tf_op jit(solution)/shard_map/all_gather | solution.py:60
  175.2 4.3 reshape.193
  179.4 5.0 fusion.28
  184.5 4.5 fusion.30
  191.1 37.4 %all-gather.15.cloned.1.call-done = bf16[16,12,6144]{2,1,0:T(8,128)(2,1)} async-done(((bf16[1,12,6144]{2,1,0:T(8,128)(2,1)}), bf16[16,12,6144]{2,1,0:T(8,128)(2,1)}) %all-gather.15.cloned.1.call-update) | async-done | bytes 2359312 | tf_op jit(solution)/shard_map/all_gather | solution.py:60
  228.6 4.3 reshape.197
  232.8 5.7 fusion.24
  238.5 10.2 %fusion.8 = f32[192,6144]{1,0:T(8,128)} fusion(bf16[1,512,6144]{2,1,0:T(8,128)(2,1)} %param.15, bf16[192,6144]{1,0:T(8,128)(2,1)} %reshape.197, bf16[1,6144,512]{2,1,0:T(8,128)(2,1)} %param.14, f32[192,512]{1,0:T(8,128)} %fusion.24), kind=kOutput, calls=%fused_computation.12 | convolution fusion | flops 2416508928 | bytes 20054016 | tf_op jit(solution)/shard_map/dot_general | solution.py:66
  248.7 9.6 %fusion.10 = f32[192,6144]{1,0:T(8,128)} fusion(bf16[1,512,6144]{2,1,0:T(8,128)(2,1)} %param.15, bf16[192,6144]{1,0:T(8,128)(2,1)S(1)} %reshape.195, bf16[1,6144,512]{2,1,0:T(8,128)(2,1)} %param.14, f32[192,512]{1,0:T(8,128)} %fusion.26), kind=kOutput, calls=%fused_computation.14 | convolution fusion | flops 2416508928 | bytes 20054016 | tf_op jit(solution)/shard_map/dot_general | solution.py:66
  258.3 10.4 %fusion.14 = f32[192,6144]{1,0:T(8,128)} fusion(bf16[1,512,6144]{2,1,0:T(8,128)(2,1)} %param.15, bf16[192,6144]{1,0:T(8,128)(2,1)} %reshape.191, bf16[1,6144,512]{2,1,0:T(8,128)(2,1)} %param.14, f32[192,512]{1,0:T(8,128)S(1)} %fusion.30), kind=kOutput, calls=%fused_computation.18 | convolution fusion | flops 2416508928 | bytes 20054016 | tf_op jit(solution)/shard_map/dot_general | solution.py:66
  268.7 9.5 %fusion.12 = f32[192,6144]{1,0:T(8,128)} fusion(bf16[1,512,6144]{2,1,0:T(8,128)(2,1)} %param.15, bf16[192,6144]{1,0:T(8,128)(2,1)S(1)} %copy-done.4, bf16[1,6144,512]{2,1,0:T(8,128)(2,1)} %param.14, f32[192,512]{1,0:T(8,128)S(1)} %fusion.28), kind=kOutput, calls=%fused_computation.16 | convolution fusion | flops 2416508928 | bytes 20054016 | tf_op jit(solution)/shard_map/dot_general | solution.py:66
  278.2 145.2 %fusion.122 = (f32[16,6144]{1,0:T(8,128)S(1)}, f32[16,6144]{1,0:T(8,128)S(1)}, f32[16,6144]{1,0:T(8,128)S(1)}, f32[16,6144]{1,0:T(8,128)S(1)}) fusion(f32[192,6144]{1,0:T(8,128)} %fusion.8, f32[192,6144]{1,0:T(8,128)} %fusion.10, f32[192,6144]{1,0:T(8,128)} %fusion.12, f32[192,6144]{1,0:T(8,128)} %fusion.14), kind=kCustom, calls=%all-reduce-scatter.4 | all-reduce-scatter fusion | flops 6291457 | bytes 20447744
  426.8 2.2 collective-permute-start.12
  430.3 5.2 collective-permute-start.15
  435.6 2.6 collective-permute-start.10
  438.2 12.9 %collective-permute-done.15 = f32[12,6144]{1,0:T(8,128)S(1)} collective-permute-done((f32[12,6144]{1,0:T(8,128)S(1)}, f32[12,6144]{1,0:T(8,128)S(1)}, u32[]{:S(2)}, u32[]{:S(2)}) %collective-permute-start.15) | collective-permute-done | bytes 294944
  453.2 6.9 %collective-permute-start.8 = (f32[16,6144]{1,0:T(8,128)S(1)}, f32[16,6144]{1,0:T(8,128)}, u32[]{:S(2)}, u32[]{:S(2)}) collective-permute-start(f32[16,6144]{1,0:T(8,128)S(1)} %get-tuple-element.17), channel_id=1, source_target_pairs={{0,1},{1,2},{2,3},{3,4},{4,5},{5,6},{6,7},{7,8},{8,9},{9,10},{10,1... | collective-permute-start | bytes 1179656
  460.1 4.8 collective-permute-start.6
  465.0 8.2 %collective-permute-start.11 = (f32[12,6144]{1,0:T(8,128)S(1)}, f32[12,6144]{1,0:T(8,128)}, u32[]{:S(2)}, u32[]{:S(2)}) collective-permute-start(f32[12,6144]{1,0:T(8,128)S(1)} %slice.122), channel_id=1, source_target_pairs={{0,4},{1,5},{2,6},{3,7},{4,8},{5,9},{6,10},{7,11},{8,12},{9,13},{1... | collective-permute-start | bytes 884744
  473.2 18.5 %concatenate.3 = f32[76,6144]{1,0:T(8,128)} concatenate(f32[12,6144]{1,0:T(8,128)} %copy-done.5, f32[16,6144]{1,0:T(8,128)S(1)} %collective-permute-done.14, f32[16,6144]{1,0:T(8,128)} %collective-permute-done.13, f32[16,6144]{1,0:T(8,128)} %collective-permute-done.12, f32[16,6144]{1,0:T(8,128)S(1)} %get-tuple-element.16), dimensions={0} | concatenate | bytes 3735552
  496.7 3.4 collective-permute-start.2
  500.1 6.9 %collective-permute-start.7 = (f32[12,6144]{1,0:T(8,128)S(1)}, f32[12,6144]{1,0:T(8,128)}, u32[]{:S(2)}, u32[]{:S(2)}) collective-permute-start(f32[12,6144]{1,0:T(8,128)S(1)} %slice.121), channel_id=1, source_target_pairs={{0,4},{1,5},{2,6},{3,7},{4,8},{5,9},{6,10},{7,11},{8,12},{9,13},{1... | collective-permute-start | bytes 884744
  507.0 18.8 %concatenate.2 = f32[76,6144]{1,0:T(8,128)} concatenate(f32[12,6144]{1,0:T(8,128)} %collective-permute-done.11, f32[16,6144]{1,0:T(8,128)} %collective-permute-done.10, f32[16,6144]{1,0:T(8,128)} %collective-permute-done.9, f32[16,6144]{1,0:T(8,128)} %collective-permute-done.8, f32[16,6144]{1,0:T(8,128)S(1)} %get-tuple-element.17), dimensions={0} | concatenate | bytes 3735552
  528.6 2.3 collective-permute-start
  530.9 3.4 collective-permute-start.3
  534.3 18.5 %concatenate.1 = f32[76,6144]{1,0:T(8,128)} concatenate(f32[12,6144]{1,0:T(8,128)} %collective-permute-done.7, f32[16,6144]{1,0:T(8,128)} %collective-permute-done.6, f32[16,6144]{1,0:T(8,128)S(1)} %collective-permute-done.5, f32[16,6144]{1,0:T(8,128)} %collective-permute-done.4, f32[16,6144]{1,0:T(8,128)S(1)} %get-tuple-element.18), dimensions={0} | concatenate | bytes 3735552
  554.0 18.3 %concatenate = f32[76,6144]{1,0:T(8,128)} concatenate(f32[12,6144]{1,0:T(8,128)} %collective-permute-done.3, f32[16,6144]{1,0:T(8,128)S(1)} %collective-permute-done.2, f32[16,6144]{1,0:T(8,128)S(1)} %collective-permute-done.1, f32[16,6144]{1,0:T(8,128)} %collective-permute-done, f32[16,6144]{1,0:T(8,128)S(1)} %get-tuple-element.19), dimensions={0} | concatenate | bytes 3735552
  584.4 44.4 %reduce-scatter.10.cloned.1.call-done = f32[4,32,768]{2,1,0:T(8,128)} async-done(((f32[4,32,6144]{2,1,0:T(8,128)}), f32[4,32,768]{2,1,0:T(8,128)}) %reduce-scatter.10.cloned.1.call-update) | async-done | bytes 393232 | tf_op jit(solution)/shard_map/reduce_scatter | solution.py:86
  (109 shorter events, 42.3 us)
Async XLA Ops:
  6.5 10.2 %copy-start = (bf16[6144,8]{0,1:T(8,128)(2,1)S(1)}, bf16[6144,8]{0,1:T(8,128)(2,1)}, u32[]{:S(2)}) copy-start(bf16[6144,8]{0,1:T(8,128)(2,1)} %param.11) | copy-start | bytes 294916
  6.5 61.5 %all-gather.13.cloned.1.call-start = ((), (), s32[]{:S(2)}) async-start(), calls=%async_computation.4 | async-start | bytes 3342336 | tf_op jit(solution)/shard_map/all_gather | solution.py:60
  10.4 6.3 copy-start.6
  13.2 108.4 %all-gather.9.cloned.1.call-start = ((), (), s32[]{:S(2)}) async-start(), calls=%async_computation.2 | async-start | bytes 3342336 | tf_op jit(solution)/shard_map/all_gather | solution.py:60
  14.7 160.4 %all-gather.11.cloned.1.call-start = ((), (), s32[]{:S(2)}) async-start(), calls=%async_computation.3 | async-start | bytes 3342336 | tf_op jit(solution)/shard_map/all_gather | solution.py:60
  15.7 212.9 %all-gather.15.cloned.1.call-start = ((), (), s32[]{:S(2)}) async-start(), calls=%async_computation.5 | async-start | bytes 3342336 | tf_op jit(solution)/shard_map/all_gather | solution.py:60
  16.6 612.3 %reduce-scatter.10.cloned.1.call-start = ((), (), s32[]{:S(2)}) async-start(), calls=%async_computation.1 | async-start | bytes 3538944 | tf_op jit(solution)/shard_map/reduce_scatter | solution.py:86
  179.4 5.0 copy-start.3
  179.4 9.5 %slice-start = ((s8[6291456]{0:T(1024)(128)(4,1)}), s8[4194304]{0:T(1024)(128)(4,1)S(1)}, s32[]{:S(2)}) async-start(s8[6291456]{0:T(1024)(128)(4,1)} %bitcast.171), calls=%async_computation.6 | async-start | bytes 8388608
  184.5 4.5 slice-start.1
  258.3 10.4 %copy-start.4 = (bf16[192,6144]{1,0:T(8,128)(2,1)S(1)}, bf16[192,6144]{1,0:T(8,128)(2,1)}, u32[]{:S(2)}) copy-start(bf16[192,6144]{1,0:T(8,128)(2,1)} %reshape.193) | copy-start | bytes 7077892
  278.2 150.8 %copy-start.7 = (u32[128]{0:T(128)S(1)}, u32[128]{0:T(128)}, u32[]{:S(2)}) copy-start(u32[128]{0:T(128)} %constant.51) | copy-start | bytes 1540
  423.4 29.8 %collective-permute-start.14 = (f32[16,6144]{1,0:T(8,128)S(1)}, f32[16,6144]{1,0:T(8,128)S(1)}, u32[]{:S(2)}, u32[]{:S(2)}) collective-permute-start(f32[16,6144]{1,0:T(8,128)S(1)} %get-tuple-element.16), channel_id=1, source_target_pairs={{0,3},{1,4},{2,5},{3,6},{4,7},{5,8},{6,9},{7,10},{8,11},{9,12},{10... | collective-permute-start | bytes 1179656
  424.7 35.4 %collective-permute-start.13 = (f32[16,6144]{1,0:T(8,128)S(1)}, f32[16,6144]{1,0:T(8,128)}, u32[]{:S(2)}, u32[]{:S(2)}) collective-permute-start(f32[16,6144]{1,0:T(8,128)S(1)} %get-tuple-element.16), channel_id=1, source_target_pairs={{0,2},{1,3},{2,4},{3,5},{4,6},{5,7},{6,8},{7,9},{8,10},{9,11},{10,... | collective-permute-start | bytes 1179656
  426.8 38.2 %collective-permute-start.12 = (f32[16,6144]{1,0:T(8,128)S(1)}, f32[16,6144]{1,0:T(8,128)}, u32[]{:S(2)}, u32[]{:S(2)}) collective-permute-start(f32[16,6144]{1,0:T(8,128)S(1)} %get-tuple-element.16), channel_id=1, source_target_pairs={{0,1},{1,2},{2,3},{3,4},{4,5},{5,6},{6,7},{7,8},{8,9},{9,10},{10,1... | collective-permute-start | bytes 1179656
  430.3 20.9 %collective-permute-start.15 = (f32[12,6144]{1,0:T(8,128)S(1)}, f32[12,6144]{1,0:T(8,128)S(1)}, u32[]{:S(2)}, u32[]{:S(2)}) collective-permute-start(f32[12,6144]{1,0:T(8,128)S(1)} %slice.123), channel_id=1, source_target_pairs={{0,4},{1,5},{2,6},{3,7},{4,8},{5,9},{6,10},{7,11},{8,12},{9,13},{1... | collective-permute-start | bytes 884744
  435.6 59.0 %collective-permute-start.10 = (f32[16,6144]{1,0:T(8,128)S(1)}, f32[16,6144]{1,0:T(8,128)}, u32[]{:S(2)}, u32[]{:S(2)}) collective-permute-start(f32[16,6144]{1,0:T(8,128)S(1)} %get-tuple-element.17), channel_id=1, source_target_pairs={{0,3},{1,4},{2,5},{3,6},{4,7},{5,8},{6,9},{7,10},{8,11},{9,12},{10... | collective-permute-start | bytes 1179656
  451.1 13.8 %copy-start.5 = (f32[12,6144]{1,0:T(8,128)}, f32[12,6144]{1,0:T(8,128)S(1)}, u32[]{:S(2)}) copy-start(f32[12,6144]{1,0:T(8,128)S(1)} %collective-permute-done.15) | copy-start | bytes 884740
  451.1 45.5 %collective-permute-start.9 = (f32[16,6144]{1,0:T(8,128)S(1)}, f32[16,6144]{1,0:T(8,128)}, u32[]{:S(2)}, u32[]{:S(2)}) collective-permute-start(f32[16,6144]{1,0:T(8,128)S(1)} %get-tuple-element.17), channel_id=1, source_target_pairs={{0,2},{1,3},{2,4},{3,5},{4,6},{5,7},{6,8},{7,9},{8,10},{9,11},{10,... | collective-permute-start | bytes 1179656
  453.2 46.9 %collective-permute-start.8 = (f32[16,6144]{1,0:T(8,128)S(1)}, f32[16,6144]{1,0:T(8,128)}, u32[]{:S(2)}, u32[]{:S(2)}) collective-permute-start(f32[16,6144]{1,0:T(8,128)S(1)} %get-tuple-element.17), channel_id=1, source_target_pairs={{0,1},{1,2},{2,3},{3,4},{4,5},{5,6},{6,7},{7,8},{8,9},{9,10},{10,1... | collective-permute-start | bytes 1179656
  460.1 68.5 %collective-permute-start.6 = (f32[16,6144]{1,0:T(8,128)S(1)}, f32[16,6144]{1,0:T(8,128)}, u32[]{:S(2)}, u32[]{:S(2)}) collective-permute-start(f32[16,6144]{1,0:T(8,128)S(1)} %get-tuple-element.18), channel_id=1, source_target_pairs={{0,3},{1,4},{2,5},{3,6},{4,7},{5,8},{6,9},{7,10},{8,11},{9,12},{10... | collective-permute-start | bytes 1179656
  465.0 27.9 %collective-permute-start.11 = (f32[12,6144]{1,0:T(8,128)S(1)}, f32[12,6144]{1,0:T(8,128)}, u32[]{:S(2)}, u32[]{:S(2)}) collective-permute-start(f32[12,6144]{1,0:T(8,128)S(1)} %slice.122), channel_id=1, source_target_pairs={{0,4},{1,5},{2,6},{3,7},{4,8},{5,9},{6,10},{7,11},{8,12},{9,13},{1... | collective-permute-start | bytes 884744
  492.8 38.1 %collective-permute-start.5 = (f32[16,6144]{1,0:T(8,128)S(1)}, f32[16,6144]{1,0:T(8,128)S(1)}, u32[]{:S(2)}, u32[]{:S(2)}) collective-permute-start(f32[16,6144]{1,0:T(8,128)S(1)} %get-tuple-element.18), channel_id=1, source_target_pairs={{0,2},{1,3},{2,4},{3,5},{4,6},{5,7},{6,8},{7,9},{8,10},{9,11},{10,... | collective-permute-start | bytes 1179656
  494.6 39.7 %collective-permute-start.4 = (f32[16,6144]{1,0:T(8,128)S(1)}, f32[16,6144]{1,0:T(8,128)}, u32[]{:S(2)}, u32[]{:S(2)}) collective-permute-start(f32[16,6144]{1,0:T(8,128)S(1)} %get-tuple-element.18), channel_id=1, source_target_pairs={{0,1},{1,2},{2,3},{3,4},{4,5},{5,6},{6,7},{7,8},{8,9},{9,10},{10,1... | collective-permute-start | bytes 1179656
  496.7 57.2 %collective-permute-start.2 = (f32[16,6144]{1,0:T(8,128)S(1)}, f32[16,6144]{1,0:T(8,128)S(1)}, u32[]{:S(2)}, u32[]{:S(2)}) collective-permute-start(f32[16,6144]{1,0:T(8,128)S(1)} %get-tuple-element.19), channel_id=1, source_target_pairs={{0,3},{1,4},{2,5},{3,6},{4,7},{5,8},{6,9},{7,10},{8,11},{9,12},{10... | collective-permute-start | bytes 1179656
  500.1 26.8 %collective-permute-start.7 = (f32[12,6144]{1,0:T(8,128)S(1)}, f32[12,6144]{1,0:T(8,128)}, u32[]{:S(2)}, u32[]{:S(2)}) collective-permute-start(f32[12,6144]{1,0:T(8,128)S(1)} %slice.121), channel_id=1, source_target_pairs={{0,4},{1,5},{2,6},{3,7},{4,8},{5,9},{6,10},{7,11},{8,12},{9,13},{1... | collective-permute-start | bytes 884744
  526.9 27.0 %collective-permute-start.1 = (f32[16,6144]{1,0:T(8,128)S(1)}, f32[16,6144]{1,0:T(8,128)S(1)}, u32[]{:S(2)}, u32[]{:S(2)}) collective-permute-start(f32[16,6144]{1,0:T(8,128)S(1)} %get-tuple-element.19), channel_id=1, source_target_pairs={{0,2},{1,3},{2,4},{3,5},{4,6},{5,7},{6,8},{7,9},{8,10},{9,11},{10,... | collective-permute-start | bytes 1179656
  528.6 25.3 %collective-permute-start = (f32[16,6144]{1,0:T(8,128)S(1)}, f32[16,6144]{1,0:T(8,128)}, u32[]{:S(2)}, u32[]{:S(2)}) collective-permute-start(f32[16,6144]{1,0:T(8,128)S(1)} %get-tuple-element.19), channel_id=1, source_target_pairs={{0,1},{1,2},{2,3},{3,4},{4,5},{5,6},{6,7},{7,8},{8,9},{9,10},{10,1... | collective-permute-start | bytes 1179656
  530.9 23.0 %collective-permute-start.3 = (f32[12,6144]{1,0:T(8,128)S(1)}, f32[12,6144]{1,0:T(8,128)}, u32[]{:S(2)}, u32[]{:S(2)}) collective-permute-start(f32[12,6144]{1,0:T(8,128)S(1)} %slice.120), channel_id=1, source_target_pairs={{0,4},{1,5},{2,6},{3,7},{4,8},{5,9},{6,10},{7,11},{8,12},{9,13},{1... | collective-permute-start | bytes 884744
  581.0 1.4 copy-start.2
  582.4 48.3 %copy-start.1 = (bf16[6144,8]{0,1:T(8,128)(2,1)S(1)}, bf16[6144,8]{0,1:T(8,128)(2,1)}, u32[]{:S(2)}) copy-start(bf16[6144,8]{0,1:T(8,128)(2,1)} %param.11) | copy-start | bytes 294916
Sparse Core Ops, SparseCore 0:
  13.3 54.7 all-gather.12
  70.5 51.0 all-gather.8
  124.1 51.0 all-gather.10
  177.5 51.0 all-gather.14
  581.2 47.6 reduce-scatter.9
where the time goes:
time: 641 us; the launch traced here: 637 us
  waiting for transfers between devices  245 us (38%)
  blocking collectives  145 us (23%)
  local copies, waits for them, and re-layouts  101 us (16%)
  matrix products  61.6 us (10%)
  starting transfers between devices  57.1 us (9%)
  between operations  14.2 us (2%)
  other arithmetic  13.3 us (2%)
    all_gather x4, waiting for transfers between devices, per_device(): piece_rows = lax.all_gather(routed, 'dp', axis=0, tiled=True)  188 us
    unnamed x1, blocking collectives  145 us
    unnamed x37, local copies, waits for them, and re-layouts  96.3 us
    unnamed x16, starting transfers between devices  56.9 us
    reduce_scatter x1, waiting for transfers between devices, per_device(): lax.psum_scatter(jnp.stack(placed), 'segment', scatter_dimension=2, tiled...  44.4 us
    dot_general x4, matrix products, per_device(): jnp.dot(hidden, down_matrix, preferred_element_type=jnp.float32)  39.7 us
    dot_general x4, matrix products, per_device(): jnp.dot(piece_rows, gate_matrix, preferred_element_type=jnp.float32)  17.3 us
    unnamed x21, waiting for transfers between devices  13 us
  transfers between devices with their start and end apart: 21, of which 6 were waited for; matrix products, arithmetic and copies ran while one was open for 14% of the time, Pallas kernels for 0%

commit v1 on v0

v1 whole, which is shorter than its diff:
```python
import functools

import jax
import jax.numpy as jnp
from jax import lax
from jax.experimental import pallas as pl
from jax.experimental.pallas import tpu as pltpu
from jax.sharding import PartitionSpec as P

MESH = pl.DeviceIdType.MESH
F32 = jnp.float32
BF16 = jnp.bfloat16
EPSILON = 1e-05

D = 6144
UNITS = 512
TOK = 128
CAP = 12
CHUNKS = 3
ROWS = 256
TILE = 768
TILES = D // TILE
STEPS = CHUNKS * TILES
RING = 8
LAG_PAIR, LAG_FAR, LAG_NEAR, LAG_ROW = 2, 5, 8, 11
HALF = D // 2


def rows_at(ref_index, count):
    return pl.ds(pl.multiple_of(ref_index, 16), count)


def kernel(
    tok_ref, gain_ref, router_ref, ids_ref, gate_hbm, up_hbm, down_hbm, out_ref,
    gate_w, up_w, down_w, normed, x_buf, hid, acc, pair_out, pair_in, chip_sum,
    first_out, far_in, second_out, near_in, row_sum, row_out, row_in, last_out, last_in,
    load_sem, ag_send, ag_recv, pair_s, pair_r, far_s, far_r, edge_s, near_s, near_r,
    row_s, row_r, last_s, last_r,
):
    s = lax.axis_index("segment")
    d = lax.axis_index("dp")
    core = d % 2
    x = (d // 2) % 4
    yh = d // 8

    def at_x(shift):
        return (s, yh * 8 + ((x + shift + 4) % 4) * 2 + core)

    across = (s, (d + 8) % 16)
    sibling = (s, yh * 8 + x * 2 + 1 - core)

    loads = [
        pltpu.make_async_copy(gate_hbm, gate_w, load_sem.at[0]),
        pltpu.make_async_copy(up_hbm, up_w, load_sem.at[1]),
        pltpu.make_async_copy(down_hbm, down_w, load_sem.at[2]),
    ]
    barrier = pltpu.get_barrier_semaphore()
    partners = [at_x(1), at_x(-1), across, sibling] + [((s + j) % 8, d) for j in range(1, 8)]
    for partner in partners:
        pl.semaphore_signal(barrier, inc=1, device_id=partner, device_id_type=MESH)
    for load in loads:
        load.start()

    def norm_rows(i, _):
        at = rows_at(i * 16, 16)
        wide = tok_ref[at, :].astype(F32)
        inverse = lax.rsqrt(jnp.mean(wide * wide, axis=-1, keepdims=True) + EPSILON)
        normed[at, :] = (wide * inverse * gain_ref[...].astype(F32)).astype(BF16)
        return 0

    lax.fori_loop(0, TOK // 16, norm_rows, 0)

    first_id = ids_ref[:, 0:1]
    second_id = ids_ref[:, 1:2]
    expert = lax.broadcasted_iota(jnp.int32, (TOK, 8), 1)
    chosen = ((first_id == expert) | (second_id == expert)).astype(F32)
    row = lax.broadcasted_iota(jnp.int32, (TOK, TOK), 0)
    col = lax.broadcasted_iota(jnp.int32, (TOK, TOK), 1)
    earlier = ((col < row) & ((col >> 5) == (row >> 5))).astype(F32)
    position = jnp.dot(
        earlier.astype(BF16), chosen.astype(BF16), preferred_element_type=F32
    )
    micro_base = ((lax.broadcasted_iota(jnp.int32, (TOK, 1), 0) >> 5) * CAP).astype(F32)
    own_slot = micro_base + jnp.sum(
        jnp.where(expert == s, position, 0.0), axis=-1, keepdims=True
    )
    named_here = (first_id == s) | (second_id == s)
    slot_range = col.astype(F32)
    placed = jnp.where(named_here & (own_slot == slot_range), 1.0, 0.0)
    dispatch = placed.T[0:48, :].astype(BF16)

    own_row = core * 128 + x * 32 + yh * 16

    def route(j, _):
        cols = pl.ds(pl.multiple_of(j * TILE, TILE), TILE)
        rows = jnp.dot(dispatch, normed[:, cols], preferred_element_type=F32).astype(BF16)
        for c in range(CHUNKS):
            x_buf[c, rows_at(own_row, 16), cols] = rows[c * 16 : (c + 1) * 16]
        return 0

    lax.fori_loop(0, TILES, route, 0)

    def pair_of(shift):
        return core * 128 + ((x + shift + 4) % 4) * 32

    low, high = pl.ds(0, HALF), pl.ds(HALF, HALF)

    def gather(c, kind):
        block = x_buf.at[c, rows_at(own_row, 16)]
        other = x_buf.at[c, rows_at(pair_of(0) + (1 - yh) * 16, 16)]
        ref, to = {
            0: lambda: (block, at_x(1)),
            1: lambda: (block, at_x(-1)),
            2: lambda: (block, across),
            3: lambda: (other, at_x(1)),
            4: lambda: (other, at_x(-1)),
            5: lambda: (x_buf.at[c, rows_at(pair_of(-1), 32), low], at_x(1)),
            6: lambda: (x_buf.at[c, rows_at(pair_of(1), 32), high], at_x(-1)),
            7: lambda: (x_buf.at[c, rows_at(pair_of(0), 32)], sibling),
            8: lambda: (x_buf.at[c, rows_at(pair_of(-1), 32)], sibling),
            9: lambda: (x_buf.at[c, rows_at(pair_of(1), 32)], sibling),
            10: lambda: (x_buf.at[c, rows_at(pair_of(2), 32)], sibling),
        }[kind]()
        return pltpu.make_async_remote_copy(
            src_ref=ref, dst_ref=ref, send_sem=ag_send.at[c, kind], recv_sem=ag_recv.at[c, kind],
            device_id=to, device_id_type=MESH,
        )

    def start_own(c):
        for kind in (2, 0, 1):
            gather(c, kind).start()

    def pass_row(c):
        gather(c, 2).wait_recv()
        for kind in (3, 4, 7):
            gather(c, kind).start()

    def pass_near(c):
        for waits, starts in (((0, 3), (5, 8)), ((1, 4), (6, 9))):
            for kind in waits:
                gather(c, kind).wait_recv()
            for kind in starts:
                gather(c, kind).start()

    def pass_far(c):
        gather(c, 5).wait_recv()
        gather(c, 6).wait_recv()
        gather(c, 10).start()

    def gathered(c):
        for kind in (7, 8, 9, 10):
            gather(c, kind).wait_recv()

    pl.semaphore_wait(barrier, len(partners))
    start_own(0)
    start_own(1)

    logits = jnp.dot(normed[...], router_ref[...], preferred_element_type=F32)
    first_logit = jnp.sum(jnp.where(expert == first_id, logits, 0.0), axis=-1, keepdims=True)
    second_logit = jnp.sum(jnp.where(expert == second_id, logits, 0.0), axis=-1, keepdims=True)
    first_gate = jax.nn.sigmoid(first_logit - second_logit)
    second_gate = jax.nn.sigmoid(second_logit - first_logit)

    pass_row(0)
    pass_near(0)
    start_own(2)
    pass_row(1)
    pass_far(0)
    pass_near(1)
    pass_row(2)
    for load in loads:
        load.wait()

    def remote(src, dst, send, recv, to):
        return pltpu.make_async_remote_copy(
            src_ref=src, dst_ref=dst, send_sem=send, recv_sem=recv, device_id=to, device_id_type=MESH
        )

    def way(n):
        return 1 - 2 * (n % 2)

    def pair_copy(n):
        return remote(pair_out.at[n % RING], pair_in.at[n], pair_s.at[n % RING], pair_r.at[n], sibling)

    def far_copy(n):
        return remote(first_out.at[n % RING, 0], far_in.at[n], far_s.at[n % RING], far_r.at[n], at_x(way(n)))

    def edge_copy(n):
        return remote(first_out.at[n % RING, 1], near_in.at[n, 1], edge_s.at[n % RING], near_r.at[n, 1], at_x(-way(n)))

    def near_copy(n):
        return remote(second_out.at[n % RING], near_in.at[n, 0], near_s.at[n % RING], near_r.at[n, 0], at_x(way(n)))

    def row_copy(n):
        return remote(row_out.at[n % RING], row_in.at[n], row_s.at[n % RING], row_r.at[n], across)

    def last_copy(n, source, to):
        c = n // TILES
        return remote(
            last_out.at[n % RING], last_in.at[c, rows_at(source * 16, 16)], last_s.at[n % RING],
            last_r.at[c, source], (to, d),
        )

    def tile_of(n):
        return (n % TILES + s + 1) % TILES

    def quarter(shift):
        return rows_at(((x + shift + 4) % 4) * 32, 32)

    def hidden_units(c):
        gathered(c)

        def part(j, _):
            cols = pl.ds(pl.multiple_of(j * 256, 256), 256)
            rows = x_buf[c]
            g = jnp.dot(rows, gate_w[:, cols], preferred_element_type=F32)
            u = jnp.dot(rows, up_w[:, cols], preferred_element_type=F32)
            hid[:, cols] = (g * jax.nn.sigmoid(g) * u).astype(BF16)
            return 0

        lax.fori_loop(0, UNITS // 256, part, 0)

    def step(n, _):
        @pl.when(n < STEPS)
        def _():
            c = n // TILES

            @pl.when(n % TILES == 0)
            def _():
                hidden_units(c)

            @pl.when(n == 0)
            def _():
                pass_far(1)
                pass_near(2)

            @pl.when(n == 4)
            def _():
                pass_far(2)

            cols = pl.ds(pl.multiple_of(tile_of(n) * TILE, TILE), TILE)
            acc[n % 3] = jnp.dot(hid[...], down_w[:, cols], preferred_element_type=F32)

            @pl.when(n >= RING)
            def _():
                pair_copy(n - RING).wait_send()

            pair_out[n % RING] = acc[n % 3, rows_at((1 - core) * 128, 128), :].astype(BF16)
            pair_copy(n).start()

        m = n - LAG_PAIR

        @pl.when((m >= 0) & (m < STEPS))
        def _():
            @pl.when(m >= RING)
            def _():
                far_copy(m - RING).wait_send()
                edge_copy(m - RING).wait_send()

            pair_copy(m).wait_recv()
            chip_sum[m % RING] = acc[m % 3, rows_at(core * 128, 128), :] + pair_in[m].astype(F32)
            first_out[m % RING, 0] = chip_sum[m % RING, quarter(2), :].astype(BF16)
            far_copy(m).start()
            first_out[m % RING, 1] = chip_sum[m % RING, quarter(-way(m)), :].astype(BF16)
            edge_copy(m).start()

        p = n - LAG_FAR

        @pl.when((p >= 0) & (p < STEPS))
        def _():
            @pl.when(p >= RING)
            def _():
                near_copy(p - RING).wait_send()

            far_copy(p).wait_recv()
            second_out[p % RING] = (
                chip_sum[p % RING, quarter(way(p)), :] + far_in[p].astype(F32)
            ).astype(BF16)
            near_copy(p).start()

        q = n - LAG_NEAR

        @pl.when((q >= 0) & (q < STEPS))
        def _():
            @pl.when(q >= RING)
            def _():
                row_copy(q - RING).wait_send()

            edge_copy(q).wait_recv()
            near_copy(q).wait_recv()
            row_sum[q % RING] = (
                chip_sum[q % RING, quarter(0), :]
                + near_in[q, 0].astype(F32)
                + near_in[q, 1].astype(F32)
            )
            row_out[q % RING] = row_sum[q % RING, rows_at((1 - yh) * 16, 16), :].astype(BF16)
            row_copy(q).start()

        r = n - LAG_ROW

        @pl.when(r >= 0)
        def _():
            row_copy(r).wait_recv()
            total = row_sum[r % RING, rows_at(yh * 16, 16), :] + row_in[r].astype(F32)

            @pl.when(r % TILES == TILES - 1)
            def _():
                last_in[r // TILES, rows_at(s * 16, 16), :] = total

            @pl.when(r % TILES != TILES - 1)
            def _():
                @pl.when(r >= RING)
                def _():
                    last_copy(r - RING, s, tile_of(r)).wait_send()

                last_out[r % RING] = total
                last_copy(r, s, tile_of(r)).start()

        return 0

    lax.fori_loop(0, STEPS + LAG_ROW, step, 0)

    position_first = jnp.sum(jnp.where(expert == first_id, position, 0.0), axis=-1, keepdims=True)
    position_second = jnp.sum(jnp.where(expert == second_id, position, 0.0), axis=-1, keepdims=True)

    def place_of(expert_id, where):
        slot = (micro_base + where).astype(jnp.int32)
        return (slot >> 4) * 128 + expert_id * 16 + (slot & 15)

    first_place = place_of(first_id, position_first)
    second_place = place_of(second_id, position_second)
    first_sum = jnp.zeros((TOK, TILE), F32)
    second_sum = jnp.zeros((TOK, TILE), F32)
    for c in range(CHUNKS):
        for j in range(1, 8):
            last_copy(c * TILES, (s + j) % 8, s).wait_recv()
        block = last_in[c]
        coarse = block.astype(BF16)
        fine = (block - coarse.astype(F32)).astype(BF16)
        pick_first = jnp.where(first_place == col + c * 128, 1.0, 0.0).astype(BF16)
        pick_second = jnp.where(second_place == col + c * 128, 1.0, 0.0).astype(BF16)
        for part in (coarse, fine):
            first_sum += jnp.dot(pick_first, part, preferred_element_type=F32)
            second_sum += jnp.dot(pick_second, part, preferred_element_type=F32)
    own_cols = pl.ds(pl.multiple_of(s * TILE, TILE), TILE)
    out_ref[...] = (
        tok_ref[:, own_cols].astype(F32) + (first_gate * first_sum + second_gate * second_sum)
    ).astype(BF16)

    for c in range(CHUNKS):
        for kind in range(11):
            gather(c, kind).wait_send()

    def drain(i, _):
        n = STEPS - RING + i
        pair_copy(n).wait_send()
        far_copy(n).wait_send()
        edge_copy(n).wait_send()
        near_copy(n).wait_send()
        row_copy(n).wait_send()

        @pl.when(i < RING - 1)
        def _():
            last_copy(n, s, tile_of(n)).wait_send()

        return 0

    lax.fori_loop(0, RING, drain, 0)


def per_device(tokens, norm_gain, router_weight, expert_ids, w_gate, w_up, w_down):
    vmem = pl.BlockSpec(memory_space=pltpu.VMEM)
    anywhere = pl.BlockSpec(memory_space=pl.ANY)
    dma = pltpu.SemaphoreType.DMA
    out = pl.pallas_call(
        kernel,
        out_shape=jax.ShapeDtypeStruct((TOK, TILE), BF16),
        in_specs=[vmem] * 4 + [anywhere] * 3,
        out_specs=vmem,
        scratch_shapes=[
            pltpu.VMEM((D, UNITS), BF16),
            pltpu.VMEM((D, UNITS), BF16),
            pltpu.VMEM((UNITS, D), BF16),
            pltpu.VMEM((TOK, D), BF16),
            pltpu.VMEM((CHUNKS, ROWS, D), BF16),
            pltpu.VMEM((ROWS, UNITS), BF16),
            pltpu.VMEM((3, ROWS, TILE), F32),
            pltpu.VMEM((RING, 128, TILE), BF16),
            pltpu.VMEM((STEPS, 128, TILE), BF16),
            pltpu.VMEM((RING, 128, TILE), F32),
            pltpu.VMEM((RING, 2, 32, TILE), BF16),
            pltpu.VMEM((STEPS, 32, TILE), BF16),
            pltpu.VMEM((RING, 32, TILE), BF16),
            pltpu.VMEM((STEPS, 2, 32, TILE), BF16),
            pltpu.VMEM((RING, 32, TILE), F32),
            pltpu.VMEM((RING, 16, TILE), BF16),
            pltpu.VMEM((STEPS, 16, TILE), BF16),
            pltpu.VMEM((RING, 16, TILE), F32),
            pltpu.VMEM((CHUNKS, 128, TILE), F32),
            dma((3,)),
            dma((CHUNKS, 11)), dma((CHUNKS, 11)),
            dma((RING,)), dma((STEPS,)),
            dma((RING,)), dma((STEPS,)),
            dma((RING,)), dma((RING,)), dma((STEPS, 2)),
            dma((RING,)), dma((STEPS,)),
            dma((RING,)), dma((CHUNKS, 8)),
        ],
        compiler_params=pltpu.CompilerParams(
            collective_id=0, has_side_effects=True, vmem_limit_bytes=61 * 2**20
        ),
        cost_estimate=pl.CostEstimate(flops=15 * 10**9, bytes_accessed=22 * 10**6, transcendentals=0),
    )(
        tokens.reshape(TOK, D), norm_gain.reshape(1, D), router_weight, expert_ids.reshape(TOK, 2),
        w_gate[0], w_up[0], w_down[0],
    )
    return out.reshape(4, 32, TILE)


def solution(mesh):
    placed = (
        P(None, "dp", None),
        P(),
        P(),
        P(None, "dp", None),
        P("segment", None, "dp"),
        P("segment", None, "dp"),
        P("segment", "dp", None),
    )
    return jax.shard_map(
        per_device, mesh=mesh, in_specs=placed, out_specs=P(None, "dp", "segment"), check_vma=False
    )
```

time: 641 us -> 115 us (0.18)
  waiting for transfers between devices: 245 us -> 0 us
  blocking collectives: 145 us -> 0 us
  Pallas kernels: 0 us -> 108 us
  local copies, waits for them, and re-layouts: 101 us -> 6.62 us
  matrix products: 61.6 us -> 0 us
  starting transfers between devices: 57.1 us -> 0 us
  between operations: 14.2 us -> 0.01 us
  other arithmetic: 13.3 us -> 0 us
    all_gather x4 -> x0, waiting for transfers between devices: 188 us -> none  [per_device(): piece_rows = lax.all_gather(routed, 'dp', axis=0, tiled=True)]
    unnamed x1 -> x0, blocking collectives: 145 us -> none
    pallas_call x0 -> x1, Pallas kernels: none -> 108 us  [per_device(): pl.pallas_call(kernel, out_shape=jax.ShapeDtypeStruct((TOK, TILE), BF16),...]
    unnamed x37 -> x3, local copies, waits for them, and re-layouts: 96.3 us -> 5.3 us
    dot_general x13 -> x0, matrix products: 61.6 us -> none  [the longest x4 39.7 us: per_device(): jnp.dot(hidden, down_matrix, preferred_element_type=jnp.float32)]
    unnamed x16 -> x0, starting transfers between devices: 56.9 us -> none
    reduce_scatter x1 -> x0, waiting for transfers between devices: 44.4 us -> none  [per_device(): lax.psum_scatter(jnp.stack(placed), 'segment', scatter_dimension=2, tiled...]
    unnamed x21 -> x0, waiting for transfers between devices: 13 us -> none
  transfers between devices with their start and end apart: 21 -> 0, of which waited for: 6 -> 0; matrix products, arithmetic and copies ran while one was open for 14% -> 0% of each run, Pallas kernels for 0% -> 0%
where the time goes in v1:
time: 115 us
  Pallas kernels  108 us (94%)
  local copies, waits for them, and re-layouts  6.62 us (6%)
    pallas_call x1, Pallas kernels, per_device(): pl.pallas_call(kernel, out_shape=jax.ShapeDtypeStruct((TOK, TILE), BF16),...  108 us
    unnamed x3, local copies, waits for them, and re-layouts  5.3 us

profile of v1, /device:TPU:0, one launch (start us, length us, event | category | flops | bytes accessed | tf_op | source)
XLA Modules:
  0.0 114.6 jit_solution(16442657121933827569)
XLA Ops:
  0.0 1.3 %reshape.13.gain_ref = bf16[1,6144]{1,0:T(2,128)(2,1)} reshape(bf16[6144]{0:T(1024)(128)(2,1)} %param.8) | data formatting | bytes 24576 | tf_op jit(solution)/shard_map/reshape | solution.py:413
  1.3 1.4 %copy.8 = s32[4,32,2]{2,1,0:T(8,128)} copy(s32[4,32,2]{1,2,0:T(2,128)} %param.10) | data formatting | bytes 2048 | tf_op args[3]
  2.7 2.3 %copy.9.router_ref = bf16[6144,8]{1,0:T(8,128)(2,1)} copy(bf16[6144,8]{0,1:T(8,128)(2,1)} %param.9) | data formatting | bytes 196608 | tf_op args[2]
  5.0 108.0 %shard_map.73 = bf16[128,768]{1,0:T(8,128)(2,1)} custom-call(bf16[128,6144]{1,0:T(8,128)(2,1)} %bitcast.11, bf16[1,6144]{1,0:T(2,128)(2,1)} %reshape.13.gain_ref, bf16[6144,8]{1,0:T(8,128)(2,1)} %copy.9.router_ref, s32[128,2]{1,0:T(8,128)} %bitcast.7, bf16[6144,512]{1,0:T(8,128)(2,1)} %bitcast.8, bf16[6144,512]{1,0:T(8,128)(2,1)} %bitcast.9, ...), custom_call_target="tpu_custom_call" | custom-call | flops 15000000512 | bytes 22000000 | tf_op jit(solution)/shard_map/pallas_call | solution.py:375
  113.0 1.6 %copy.11 = bf16[4,32,768]{2,1,0:T(8,128)(2,1)} copy(bf16[4,32,768]{2,1,0:T(8,128)(2,1)} %bitcast.6) | data formatting | bytes 393216

commit v2 on v1

v2 whole, which is shorter than its diff:
```python
import functools

import jax
import jax.numpy as jnp
from jax import lax
from jax.experimental import pallas as pl
from jax.experimental.pallas import tpu as pltpu
from jax.sharding import PartitionSpec as P

MESH = pl.DeviceIdType.MESH
F32 = jnp.float32
BF16 = jnp.bfloat16
EPSILON = 1e-05

D = 6144
UNITS = 512
TOK = 128
CAP = 12
CHUNKS = 3
ROWS = 256
TILE = 768
TILES = D // TILE
STEPS = CHUNKS * TILES
RING = 8
KEEP = 12
LAG_PAIR, LAG_FAR, LAG_NEAR, LAG_ROW = 2, 6, 10, 14
HALF = D // 2
LATE = 2560
MIDDLE = (D + LATE) // 2
ROW_TILES = 2


def rows_at(ref_index, count):
    return pl.ds(pl.multiple_of(ref_index, 16), count)


def kernel(
    tok_ref, gain_ref, router_ref, ids_ref, gate_hbm, up_hbm, down_hbm, out_ref,
    gate_w, up_w, down_w, normed, x_buf, hid, acc, pair_out, pair_in, chip_sum,
    first_out, far_in, second_out, near_in, row_sum, row_out, row_in, rows_out, rows_in,
    last_out, last_in, scored,
    load_sem, ag_send, ag_recv, pair_s, pair_r, far_s, far_r, edge_s, near_s, near_r,
    row_s, row_r, rows_s, rows_r, last_s, last_r,
):
    s = lax.axis_index("segment")
    d = lax.axis_index("dp")
    core = d % 2
    x = (d // 2) % 4
    yh = d // 8

    def at_x(shift):
        return (s, yh * 8 + ((x + shift + 4) % 4) * 2 + core)

    across = (s, (d + 8) % 16)
    sibling = (s, yh * 8 + x * 2 + 1 - core)

    loads = [
        pltpu.make_async_copy(gate_hbm, gate_w, load_sem.at[0]),
        pltpu.make_async_copy(up_hbm, up_w, load_sem.at[1]),
        pltpu.make_async_copy(down_hbm, down_w, load_sem.at[2]),
    ]
    barrier = pltpu.get_barrier_semaphore()
    partners = [at_x(1), at_x(-1), across, sibling] + [((s + j) % 8, d) for j in range(1, 8)]
    for partner in partners:
        pl.semaphore_signal(barrier, inc=1, device_id=partner, device_id_type=MESH)
    for load in loads:
        load.start()

    def id_column(which):
        eye = lax.broadcasted_iota(jnp.int32, (32, 32), 0) == lax.broadcasted_iota(
            jnp.int32, (32, 32), 1
        )
        columns = [
            jnp.sum(
                jnp.where(eye, ids_ref[m, which : which + 1, :].astype(F32), 0.0),
                axis=-1,
                keepdims=True,
            )
            for m in range(4)
        ]
        return jnp.concatenate(columns, axis=0).astype(jnp.int32)

    first_id = id_column(0)
    second_id = id_column(1)
    expert = lax.broadcasted_iota(jnp.int32, (TOK, 8), 1)
    chosen = ((first_id == expert) | (second_id == expert)).astype(F32)
    row = lax.broadcasted_iota(jnp.int32, (TOK, TOK), 0)
    col = lax.broadcasted_iota(jnp.int32, (TOK, TOK), 1)
    earlier = ((col < row) & ((col >> 5) == (row >> 5))).astype(F32)
    position = jnp.dot(
        earlier.astype(BF16), chosen.astype(BF16), preferred_element_type=F32
    )
    micro_base = ((lax.broadcasted_iota(jnp.int32, (TOK, 1), 0) >> 5) * CAP).astype(F32)
    own_slot = micro_base + jnp.sum(
        jnp.where(expert == s, position, 0.0), axis=-1, keepdims=True
    )
    named_here = (first_id == s) | (second_id == s)
    slot_range = col.astype(F32)
    dispatch = jnp.where(named_here & (own_slot == slot_range), 1.0, 0.0).T

    def norm(first, count):
        gain = gain_ref[...].astype(F32).reshape(1, D)

        def norm_rows(i, _):
            at = rows_at(first + i * 16, 16)
            wide = tok_ref[at, :].astype(F32)
            inverse = lax.rsqrt(jnp.mean(wide * wide, axis=-1, keepdims=True) + EPSILON)
            normed[at, :] = (wide * inverse * gain).astype(BF16)
            return 0

        lax.fori_loop(0, count // 16, norm_rows, 0)

    own_row = core * 128 + x * 32 + yh * 16

    def route(c):
        pick = dispatch[c * 16 : (c + 1) * 16, c * 32 : c * 32 + 64].astype(BF16)

        def columns(j, _):
            cols = pl.ds(pl.multiple_of(j * TILE, TILE), TILE)
            x_buf[c, rows_at(own_row, 16), cols] = jnp.dot(
                pick, normed[c * 32 : c * 32 + 64, cols], preferred_element_type=F32
            ).astype(BF16)
            return 0

        lax.fori_loop(0, TILES, columns, 0)

    def pair_of(shift):
        return core * 128 + ((x + shift + 4) % 4) * 32

    def gather(c, kind):
        def block(shift, row):
            return x_buf.at[c, rows_at(pair_of(shift) + row * 16, 16)]

        def part(shift, row, start, stop):
            return x_buf.at[c, rows_at(pair_of(shift) + row * 16, 16), pl.ds(start, stop - start)]

        def pair(shift):
            return x_buf.at[c, rows_at(pair_of(shift), 32)]

        ref, to = {
            0: lambda: (block(0, yh), at_x(1)),
            1: lambda: (block(0, yh), at_x(-1)),
            2: lambda: (block(0, yh), across),
            3: lambda: (part(0, 1 - yh, LATE, D), at_x(1)),
            4: lambda: (part(0, 1 - yh, LATE, D), at_x(-1)),
            5: lambda: (part(-1, yh, 0, HALF), at_x(1)),
            6: lambda: (part(1, yh, HALF, D), at_x(-1)),
            7: lambda: (part(-1, 1 - yh, LATE, MIDDLE), at_x(1)),
            8: lambda: (part(1, 1 - yh, MIDDLE, D), at_x(-1)),
            9: lambda: (part(-1, yh, 0, LATE), across),
            10: lambda: (part(1, yh, 0, LATE), across),
            11: lambda: (part(2, yh, 0, LATE), across),
            12: lambda: (pair(0), sibling),
            13: lambda: (pair(-1), sibling),
            14: lambda: (pair(1), sibling),
            15: lambda: (pair(2), sibling),
        }[kind]()
        return pltpu.make_async_remote_copy(
            src_ref=ref, dst_ref=ref, send_sem=ag_send.at[c, kind], recv_sem=ag_recv.at[c, kind],
            device_id=to, device_id_type=MESH,
        )

    def go_on(c, waits, starts):
        for kind in waits:
            gather(c, kind).wait_recv()
        for kind in starts:
            gather(c, kind).start()

    def own_rows(c):
        go_on(c, (), (0, 1, 2))

    def pass_first(c):
        go_on(c, (0,), (5, 9))
        go_on(c, (1,), (6, 10))
        go_on(c, (2,), (3, 4, 12))

    def pass_near(c):
        go_on(c, (3,), (7,))
        go_on(c, (4,), (8,))
        go_on(c, (5, 6), (11,))

    def pass_late(c):
        go_on(c, (9,), (13,))
        go_on(c, (10,), (14,))

    def pass_far(c):
        go_on(c, (7, 8, 11), (15,))

    def gathered(c):
        go_on(c, (12, 13, 14, 15), ())

    norm(0, 64)
    route(0)
    pl.semaphore_wait(barrier, len(partners))
    own_rows(0)
    norm(64, 32)
    route(1)
    own_rows(1)
    norm(96, 32)
    route(2)

    logits = lax.dot_general(
        normed[...], router_ref[...], (((1,), (1,)), ((), ())), preferred_element_type=F32
    )
    first_logit = jnp.sum(jnp.where(expert == first_id, logits, 0.0), axis=-1, keepdims=True)
    second_logit = jnp.sum(jnp.where(expert == second_id, logits, 0.0), axis=-1, keepdims=True)
    first_gate = jax.nn.sigmoid(first_logit - second_logit)
    second_gate = jax.nn.sigmoid(second_logit - first_logit)

    pass_first(0)
    pass_near(0)
    pass_first(1)
    own_rows(2)
    pass_late(0)
    pass_far(0)
    pass_near(1)
    for load in loads:
        load.wait()

    def remote(src, dst, send, recv, to):
        return pltpu.make_async_remote_copy(
            src_ref=src, dst_ref=dst, send_sem=send, recv_sem=recv, device_id=to, device_id_type=MESH
        )

    def way(n):
        return 1 - 2 * (n % 2)

    def pair_copy(n):
        return remote(pair_out.at[n % RING], pair_in.at[n], pair_s.at[n % RING], pair_r.at[n], sibling)

    def far_copy(n):
        return remote(first_out.at[n % RING, 0], far_in.at[n], far_s.at[n % RING], far_r.at[n], at_x(way(n)))

    def edge_copy(n):
        return remote(first_out.at[n % RING, 1], near_in.at[n, 1], edge_s.at[n % RING], near_r.at[n, 1], at_x(-way(n)))

    def near_copy(n):
        return remote(second_out.at[n % RING], near_in.at[n, 0], near_s.at[n % RING], near_r.at[n, 0], at_x(way(n)))

    def row_copy(n):
        return remote(row_out.at[n % RING], row_in.at[n], row_s.at[n % RING], row_r.at[n], across)

    def row_first(n):
        return (n % TILES == 2) | (n % TILES == 5)

    def row_place(n):
        return (n // TILES) * ROW_TILES + (n % TILES) // 4

    def rows_copy(n):
        return remote(rows_out.at[(n % TILES) // 4], rows_in.at[row_place(n)], rows_s.at[(n % TILES) // 4], rows_r.at[row_place(n)], across)

    top = pl.ds(0, 16)

    def far_block(n):
        return remote(first_out.at[n % RING, 0, top], far_in.at[n, top], far_s.at[n % RING], far_r.at[n], at_x(way(n)))

    def edge_block(n):
        return remote(first_out.at[n % RING, 1, top], near_in.at[n, 1, top], edge_s.at[n % RING], near_r.at[n, 1], at_x(-way(n)))

    def near_block(n):
        return remote(second_out.at[n % RING, top], near_in.at[n, 0, top], near_s.at[n % RING], near_r.at[n, 0], at_x(way(n)))

    def last_copy(n, source, to):
        c = n // TILES
        return remote(
            last_out.at[n % RING], last_in.at[c, rows_at(source * 16, 16)], last_s.at[n % RING],
            last_r.at[c, source], (to, d),
        )

    def tile_of(n):
        return (n % TILES + s + 1) % TILES

    def quarter(shift):
        return rows_at(((x + shift + 4) % 4) * 32, 32)

    def own_block(shift):
        return rows_at(((x + shift + 4) % 4) * 32 + yh * 16, 16)

    def hidden_units(c):
        gathered(c)

        def part(j, _):
            cols = pl.ds(pl.multiple_of(j * 256, 256), 256)
            rows = x_buf[c]
            g = jnp.dot(rows, gate_w[:, cols], preferred_element_type=F32)
            u = jnp.dot(rows, up_w[:, cols], preferred_element_type=F32)
            hid[:, cols] = (g * jax.nn.sigmoid(g) * u).astype(BF16)
            return 0

        lax.fori_loop(0, UNITS // 256, part, 0)

    def place_of(expert_id):
        where = jnp.sum(jnp.where(expert == expert_id, position, 0.0), axis=-1, keepdims=True)
        slot = (micro_base + where).astype(jnp.int32)
        return (slot >> 4) * 128 + expert_id * 16 + (slot & 15)

    first_place = place_of(first_id)
    second_place = place_of(second_id)
    own_cols = pl.ds(pl.multiple_of(s * TILE, TILE), TILE)
    scored[...] = tok_ref[:, own_cols].astype(F32)

    def combine(c):
        for j in range(1, 8):
            last_copy(c * TILES, (s + j) % 8, s).wait_recv()
        block = last_in[c]
        coarse = block.astype(BF16)
        fine = (block - coarse.astype(F32)).astype(BF16)
        toks = slice(c * 32, c * 32 + 64)
        added = 0.0
        for place, gate in ((first_place, first_gate), (second_place, second_gate)):
            pick = jnp.where(place == col + c * 128, 1.0, 0.0)[toks].astype(BF16)
            added += gate[toks] * (
                jnp.dot(pick, coarse, preferred_element_type=F32)
                + jnp.dot(pick, fine, preferred_element_type=F32)
            )
        scored[toks] += added

    def step(n, _):
        @pl.when(n < STEPS)
        def _():
            c = n // TILES

            @pl.when(n % TILES == 0)
            def _():
                hidden_units(c)

            @pl.when(n == 0)
            def _():
                pass_late(1)
                pass_far(1)

            @pl.when(n == 2)
            def _():
                pass_first(2)

            @pl.when(n == 6)
            def _():
                pass_near(2)

            @pl.when(n == 11)
            def _():
                pass_late(2)
                pass_far(2)

            cols = pl.ds(pl.multiple_of(tile_of(n) * TILE, TILE), TILE)
            acc[n % 3] = jnp.dot(hid[...], down_w[:, cols], preferred_element_type=F32)

            @pl.when(n >= RING)
            def _():
                pair_copy(n - RING).wait_send()

            pair_out[n % RING] = acc[n % 3, rows_at((1 - core) * 128, 128), :].astype(BF16)
            pair_copy(n).start()

        m = n - LAG_PAIR

        @pl.when((m >= 0) & (m < STEPS))
        def _():
            slot = m % RING
            pair_copy(m).wait_recv()
            chip_sum[m % KEEP] = acc[m % 3, rows_at(core * 128, 128), :] + pair_in[m].astype(F32)

            @pl.when(row_first(m))
            def _():
                @pl.when(m >= RING)
                def _():
                    rows_copy(m - RING).wait_send()

                for i in range(4):
                    rows_out[(m % TILES) // 4, i] = chip_sum[m % KEEP, rows_at(i * 32 + (1 - yh) * 16, 16), :].astype(BF16)
                rows_copy(m).start()

            @pl.when(jnp.logical_not(row_first(m)))
            def _():
                @pl.when(m >= RING)
                def _():
                    far_copy(m - RING).wait_send()
                    edge_copy(m - RING).wait_send()

                first_out[slot, 0] = chip_sum[m % KEEP, quarter(2), :].astype(BF16)
                far_copy(m).start()
                first_out[slot, 1] = chip_sum[m % KEEP, quarter(-way(m)), :].astype(BF16)
                edge_copy(m).start()

        p = n - LAG_FAR

        @pl.when((p >= 0) & (p < STEPS))
        def _():
            slot = p % RING

            @pl.when(row_first(p))
            def _():
                @pl.when(p >= RING)
                def _():
                    far_block(p - RING).wait_send()
                    edge_block(p - RING).wait_send()

                rows_copy(p).wait_recv()
                for i in range(4):
                    chip_sum[p % KEEP, rows_at(i * 32 + yh * 16, 16), :] += rows_in[row_place(p), i].astype(F32)
                first_out[slot, 0, top] = chip_sum[p % KEEP, own_block(2), :].astype(BF16)
                far_block(p).start()
                first_out[slot, 1, top] = chip_sum[p % KEEP, own_block(-way(p)), :].astype(BF16)
                edge_block(p).start()

            @pl.when(jnp.logical_not(row_first(p)))
            def _():
                @pl.when(p >= RING)
                def _():
                    near_copy(p - RING).wait_send()

                far_copy(p).wait_recv()
                second_out[slot] = (
                    chip_sum[p % KEEP, quarter(way(p)), :] + far_in[p].astype(F32)
                ).astype(BF16)
                near_copy(p).start()

        q = n - LAG_NEAR

        @pl.when((q >= 0) & (q < STEPS))
        def _():
            slot = q % RING

            @pl.when(row_first(q))
            def _():
                @pl.when(q >= RING)
                def _():
                    near_block(q - RING).wait_send()

                far_block(q).wait_recv()
                second_out[slot, top] = (
                    chip_sum[q % KEEP, own_block(way(q)), :] + far_in[q, top].astype(F32)
                ).astype(BF16)
                near_block(q).start()
                row_sum[slot, top] = chip_sum[q % KEEP, own_block(0), :]

            @pl.when(jnp.logical_not(row_first(q)))
            def _():
                @pl.when(q >= RING)
                def _():
                    row_copy(q - RING).wait_send()

                edge_copy(q).wait_recv()
                near_copy(q).wait_recv()
                row_sum[slot] = (
                    chip_sum[q % KEEP, quarter(0), :]
                    + near_in[q, 0].astype(F32)
                    + near_in[q, 1].astype(F32)
                )
                row_out[slot] = row_sum[slot, rows_at((1 - yh) * 16, 16), :].astype(BF16)
                row_copy(q).start()

        r = n - LAG_ROW

        @pl.when(r >= 0)
        def _():
            slot = r % RING

            def hand_out(total):
                @pl.when(r >= RING)
                def _():
                    last_copy(r - RING, s, tile_of(r)).wait_send()

                last_out[slot] = total
                last_copy(r, s, tile_of(r)).start()

            @pl.when(row_first(r))
            def _():
                edge_block(r).wait_recv()
                near_block(r).wait_recv()
                hand_out(
                    row_sum[slot, top] + near_in[r, 0, top].astype(F32) + near_in[r, 1, top].astype(F32)
                )

            @pl.when(jnp.logical_not(row_first(r)))
            def _():
                row_copy(r).wait_recv()
                total = row_sum[slot, rows_at(yh * 16, 16), :] + row_in[r].astype(F32)

                @pl.when(r % TILES == TILES - 1)
                def _():
                    last_in[r // TILES, rows_at(s * 16, 16), :] = total

                @pl.when(r % TILES != TILES - 1)
                def _():
                    hand_out(total)

        for c in range(CHUNKS - 1):

            @pl.when(n == (c + 1) * TILES + LAG_ROW + 3)
            def _():
                combine(c)

        return 0

    lax.fori_loop(0, STEPS + LAG_ROW, step, 0)

    combine(CHUNKS - 1)
    out_ref[...] = scored[...].astype(BF16)

    for c in range(CHUNKS):
        for kind in range(16):
            gather(c, kind).wait_send()

    def drain(i, _):
        n = STEPS - RING + i
        pair_copy(n).wait_send()

        @pl.when(row_first(n))
        def _():
            rows_copy(n).wait_send()
            far_block(n).wait_send()
            edge_block(n).wait_send()
            near_block(n).wait_send()

        @pl.when(jnp.logical_not(row_first(n)))
        def _():
            far_copy(n).wait_send()
            edge_copy(n).wait_send()
            near_copy(n).wait_send()
            row_copy(n).wait_send()

        @pl.when(i < RING - 1)
        def _():
            last_copy(n, s, tile_of(n)).wait_send()

        return 0

    lax.fori_loop(0, RING, drain, 0)


def per_device(tokens, norm_gain, router_weight, expert_ids, w_gate, w_up, w_down):
    vmem = pl.BlockSpec(memory_space=pltpu.VMEM)
    anywhere = pl.BlockSpec(memory_space=pl.ANY)
    dma = pltpu.SemaphoreType.DMA
    out = pl.pallas_call(
        kernel,
        out_shape=jax.ShapeDtypeStruct((TOK, TILE), BF16),
        in_specs=[vmem] * 4 + [anywhere] * 3,
        out_specs=vmem,
        scratch_shapes=[
            pltpu.VMEM((D, UNITS), BF16),
            pltpu.VMEM((D, UNITS), BF16),
            pltpu.VMEM((UNITS, D), BF16),
            pltpu.VMEM((TOK, D), BF16),
            pltpu.VMEM((CHUNKS, ROWS, D), BF16),
            pltpu.VMEM((ROWS, UNITS), BF16),
            pltpu.VMEM((3, ROWS, TILE), F32),
            pltpu.VMEM((RING, 128, TILE), BF16),
            pltpu.VMEM((STEPS, 128, TILE), BF16),
            pltpu.VMEM((KEEP, 128, TILE), F32),
            pltpu.VMEM((RING, 2, 32, TILE), BF16),
            pltpu.VMEM((STEPS, 32, TILE), BF16),
            pltpu.VMEM((RING, 32, TILE), BF16),
            pltpu.VMEM((STEPS, 2, 32, TILE), BF16),
            pltpu.VMEM((RING, 32, TILE), F32),
            pltpu.VMEM((RING, 16, TILE), BF16),
            pltpu.VMEM((STEPS, 16, TILE), BF16),
            pltpu.VMEM((ROW_TILES, 4, 16, TILE), BF16),
            pltpu.VMEM((CHUNKS * ROW_TILES, 4, 16, TILE), BF16),
            pltpu.VMEM((RING, 16, TILE), F32),
            pltpu.VMEM((CHUNKS, 128, TILE), F32),
            pltpu.VMEM((TOK, TILE), F32),
            dma((3,)),
            dma((CHUNKS, 16)), dma((CHUNKS, 16)),
            dma((RING,)), dma((STEPS,)),
            dma((RING,)), dma((STEPS,)),
            dma((RING,)), dma((RING,)), dma((STEPS, 2)),
            dma((RING,)), dma((STEPS,)),
            dma((ROW_TILES,)), dma((CHUNKS * ROW_TILES,)),
            dma((RING,)), dma((CHUNKS, 8)),
        ],
        compiler_params=pltpu.CompilerParams(
            collective_id=0, has_side_effects=True, vmem_limit_bytes=61 * 2**20
        ),
        cost_estimate=pl.CostEstimate(flops=15 * 10**9, bytes_accessed=22 * 10**6, transcendentals=0),
    )(
        tokens.reshape(TOK, D), norm_gain, router_weight.T, expert_ids.transpose(0, 2, 1),
        w_gate[0], w_up[0], w_down[0],
    )
    return out.reshape(4, 32, TILE)


def solution(mesh):
    placed = (
        P(None, "dp", None),
        P(),
        P(),
        P(None, "dp", None),
        P("segment", None, "dp"),
        P("segment", None, "dp"),
        P("segment", "dp", None),
    )
    return jax.shard_map(
        per_device, mesh=mesh, in_specs=placed, out_specs=P(None, "dp", "segment"), check_vma=False
    )
```

time: 115 us -> 96.2 us (0.84)
  Pallas kernels: 108 us -> 94.4 us
  local copies, waits for them, and re-layouts: 6.62 us -> 1.62 us
    pallas_call x1, Pallas kernels: 108 us -> 94.4 us  [per_device(): pl.pallas_call(kernel, out_shape=jax.ShapeDtypeStruct((TOK, TILE), BF16),...]
    unnamed x3 -> x1, local copies, waits for them, and re-layouts: 5.3 us -> 1.62 us
    reshape x1 -> x0, local copies, waits for them, and re-layouts: 1.32 us -> none  [per_device(): norm_gain.reshape(1, D)]
where the time goes in v2:
time: 96.2 us; the launch traced here: 96 us
  Pallas kernels  94.4 us (98%)
  local copies, waits for them, and re-layouts  1.62 us (2%)
    pallas_call x1, Pallas kernels, per_device(): pl.pallas_call(kernel, out_shape=jax.ShapeDtypeStruct((TOK, TILE), BF16),...  94.4 us

profile of v2, /device:TPU:0, one launch (start us, length us, event | category | flops | bytes accessed | tf_op | source)
XLA Modules:
  0.0 96.0 jit_solution(12398938192885530643)
XLA Ops:
  0.0 94.4 %shard_map.73 = bf16[128,768]{1,0:T(8,128)(2,1)} custom-call(bf16[128,6144]{1,0:T(8,128)(2,1)} %bitcast.11, bf16[6144]{0:T(1024)(128)(2,1)} %gain_ref.1, bf16[8,6144]{1,0:T(8,128)(2,1)} %bitcast.12, s32[4,2,32]{2,1,0:T(2,128)} %bitcast.13, bf16[6144,512]{1,0:T(8,128)(2,1)} %bitcast.8, bf16[6144,512]{1,0:T(8,128)(2,1)} %bitcast.9, bf16[512,6144]{1,0:T(8,128)(2,1)} %bitcast.10), custom_call_target="tpu_custom_call" | custom-call | flops 15000000512 | bytes 22000000 | tf_op jit(solution)/shard_map/pallas_call | solution.py:536
  94.4 1.6 %copy.9 = bf16[4,32,768]{2,1,0:T(8,128)(2,1)} copy(bf16[4,32,768]{2,1,0:T(8,128)(2,1)} %bitcast.7) | data formatting | bytes 393216

commit v3 on v2

--- a/solution.py
+++ b/solution.py
@@ -195,7 +195,6 @@
     own_rows(0)
     norm(64, 32)
     route(1)
-    own_rows(1)
     norm(96, 32)
     route(2)
 
@@ -208,12 +207,13 @@
     second_gate = jax.nn.sigmoid(second_logit - first_logit)
 
     pass_first(0)
+    own_rows(1)
     pass_near(0)
+    pass_late(0)
+    pass_far(0)
     pass_first(1)
     own_rows(2)
-    pass_late(0)
-    pass_far(0)
-    pass_near(1)
+
     for load in loads:
         load.wait()
 
@@ -326,18 +326,22 @@
 
             @pl.when(n == 0)
             def _():
+                pass_near(1)
+
+            @pl.when(n == 3)
+            def _():
                 pass_late(1)
                 pass_far(1)
 
-            @pl.when(n == 2)
+            @pl.when(n == 5)
             def _():
                 pass_first(2)
 
-            @pl.when(n == 6)
+            @pl.when(n == 9)
             def _():
                 pass_near(2)
 
-            @pl.when(n == 11)
+            @pl.when(n == 13)
             def _():
                 pass_late(2)
                 pass_far(2)

time: 96.2 us -> 93.1 us (0.968)
  Pallas kernels: 94.4 us -> 91.4 us
    pallas_call x1, Pallas kernels: 94.4 us -> 91.4 us  [per_device(): pl.pallas_call(kernel, out_shape=jax.ShapeDtypeStruct((TOK, TILE), BF16),...]
where the time goes in v3:
time: 93.1 us; the launch traced here: 93 us
  Pallas kernels  91.4 us (98%)
  local copies, waits for them, and re-layouts  1.62 us (2%)
    pallas_call x1, Pallas kernels, per_device(): pl.pallas_call(kernel, out_shape=jax.ShapeDtypeStruct((TOK, TILE), BF16),...  91.4 us

profile of v3, /device:TPU:0, one launch (start us, length us, event | category | flops | bytes accessed | tf_op | source)
XLA Modules:
  0.0 93.0 jit_solution(16150176453601598110)
XLA Ops:
  0.0 91.4 %shard_map.73 = bf16[128,768]{1,0:T(8,128)(2,1)} custom-call(bf16[128,6144]{1,0:T(8,128)(2,1)} %bitcast.11, bf16[6144]{0:T(1024)(128)(2,1)} %gain_ref.1, bf16[8,6144]{1,0:T(8,128)(2,1)} %bitcast.12, s32[4,2,32]{2,1,0:T(2,128)} %bitcast.13, bf16[6144,512]{1,0:T(8,128)(2,1)} %bitcast.8, bf16[6144,512]{1,0:T(8,128)(2,1)} %bitcast.9, bf16[512,6144]{1,0:T(8,128)(2,1)} %bitcast.10), custom_call_target="tpu_custom_call" | custom-call | flops 15000000512 | bytes 22000000 | tf_op jit(solution)/shard_map/pallas_call | solution.py:540
  91.4 1.6 %copy.9 = bf16[4,32,768]{2,1,0:T(8,128)(2,1)} copy(bf16[4,32,768]{2,1,0:T(8,128)(2,1)} %bitcast.7) | data formatting | bytes 393216

commit v4 on v3

--- a/solution.py
+++ b/solution.py
@@ -170,9 +170,9 @@
         go_on(c, (), (0, 1, 2))
 
     def pass_first(c):
+        go_on(c, (2,), (3, 4, 12))
         go_on(c, (0,), (5, 9))
         go_on(c, (1,), (6, 10))
-        go_on(c, (2,), (3, 4, 12))
 
     def pass_near(c):
         go_on(c, (3,), (7,))

time: 93.1 us -> 93.4 us (level)
  no operation moved by 1% of the time
where the time goes in v4:
time: 93.4 us; the launch traced here: 93.2 us
  Pallas kernels  91.6 us (98%)
  local copies, waits for them, and re-layouts  1.62 us (2%)
    pallas_call x1, Pallas kernels, per_device(): pl.pallas_call(kernel, out_shape=jax.ShapeDtypeStruct((TOK, TILE), BF16),...  91.6 us

profile of v4, /device:TPU:0, one launch (start us, length us, event | category | flops | bytes accessed | tf_op | source)
XLA Modules:
  0.0 93.2 jit_solution(9047762007328655680)
XLA Ops:
  0.0 91.6 %shard_map.73 = bf16[128,768]{1,0:T(8,128)(2,1)} custom-call(bf16[128,6144]{1,0:T(8,128)(2,1)} %bitcast.11, bf16[6144]{0:T(1024)(128)(2,1)} %gain_ref.1, bf16[8,6144]{1,0:T(8,128)(2,1)} %bitcast.12, s32[4,2,32]{2,1,0:T(2,128)} %bitcast.13, bf16[6144,512]{1,0:T(8,128)(2,1)} %bitcast.8, bf16[6144,512]{1,0:T(8,128)(2,1)} %bitcast.9, bf16[512,6144]{1,0:T(8,128)(2,1)} %bitcast.10), custom_call_target="tpu_custom_call" | custom-call | flops 15000000512 | bytes 22000000 | tf_op jit(solution)/shard_map/pallas_call | solution.py:540
  91.6 1.6 %copy.9 = bf16[4,32,768]{2,1,0:T(8,128)(2,1)} copy(bf16[4,32,768]{2,1,0:T(8,128)(2,1)} %bitcast.7) | data formatting | bytes 393216
